TPU v7x, 32 devices: a whole 2x2x4 slice. The times are simulated.
32 devices in a mesh: tm: 4 (over y, x), tile: 8 (over z, core).
Axes of the slice: x: 2, y: 2, z: 4, core: 2. Of those that a mesh axis runs over, the one named last changes fastest.
Arguments:
- first_input: bfloat16 [8, 32, 32, 384], P('tm', None, 'tile'), may hold values from -6 to 6
- second_input: bfloat16 [8, 32, 32, 384], P('tm', None, 'tile'), may hold values from -6 to 6
- output_grad: bfloat16 [8, 32, 32, 384], P('tm', None, 'tile'), may hold values from -6 to 6
- first_gain: float32 [384], replicated, may hold values from 0.1 to 1.9
- first_shift: float32 [384], replicated, may hold values from -1 to 1
- first_kernel: bfloat16 [27, 384, 384], replicated, may hold values from -1 to 1
- second_gain: float32 [384], replicated, may hold values from 0.1 to 1.9
- second_shift: float32 [384], replicated, may hold values from -1 to 1
- second_kernel: bfloat16 [27, 384, 384], replicated, may hold values from -1 to 1
- latent_kernel: bfloat16 [27, 16, 384], replicated, may hold values from -0.0625 to 0.0625
Outputs:
- latent_grad: float32 [64, 2048], P(None, ('tm', 'tile'))
All inputs are finite; a program needn't handle non-finite values.
Results may differ from a plain program's by a relative error of at most 0.0044.
Values may be sent and summed in bfloat16 or wider, within the bound.
A program may use at most 64 MiB of HBM per device.

v0:
```python
import functools

import jax
import jax.numpy as jnp
import ml_dtypes
import numpy as np
from jax import lax
from jax.experimental import pallas as pl
from jax.experimental.pallas import tpu as pltpu
from jax.sharding import PartitionSpec as P

GROUPS = 32
MESH = pl.DeviceIdType.MESH
epsilon = 1e-05
NT = (((1,), (1,)), ((), ()))


def split3(value):
    hi = value.astype(jnp.bfloat16).astype(jnp.float32)
    rest = value - hi
    mid = rest.astype(jnp.bfloat16).astype(jnp.float32)
    return hi, mid, rest - mid


def times_exact(value, ones):
    rows = value.shape[0]
    parts = jnp.concatenate(split3(value), axis=0).astype(jnp.bfloat16)
    out = jnp.dot(parts, ones, preferred_element_type=jnp.float32)
    return out[:rows] + out[rows : 2 * rows] + out[2 * rows :]


def body(
    n_tm, n,
    x2_ref, x1_ref, g_ref, gain2, shift2, gain1, shift1, lat_ref,
    k2_hbm, k1_hbm, group_hbm, place_hbm,
    out_ref,
    g1, g2, g3, kb2, kb1, group_m, place_m, acc, xhat_s, coef_s, q_s,
    mom, sums2, sums1, outgoing, incoming,
    k_sem, c_sem, halo_send, halo_recv, st_send, st_recv, a_send, a_recv,
):
    tm = lax.axis_index("tm")
    me = lax.axis_index("tile")
    frames, cols, rows, chans = x2_ref.shape
    lat = lat_ref.shape[1]
    spot = cols * rows
    area = frames * spot
    cells = float(rows * cols * n * (chans // GROUPS))
    has_l, has_r = me > 0, me < n - 1
    has_p, has_f = tm > 0, tm < n_tm - 1
    f32 = jnp.float32

    def load(src, dst, which, a, c):
        return pltpu.make_async_copy(
            src.at[pl.ds(3 * a, 3), c],
            dst.at[pl.ds(3 * a, 3), :, pl.ds(c * chans, chans)],
            k_sem.at[which, a, c],
        )

    const_loads = [
        pltpu.make_async_copy(group_hbm, group_m, c_sem.at[0]),
        pltpu.make_async_copy(place_hbm, place_m, c_sem.at[1]),
    ]
    const_loads[0].start()
    for a in (2, 1, 0):
        for c in range(3):
            load(k2_hbm, kb2, 0, a, c).start()
    for a in (2, 1, 0):
        for c in range(3):
            load(k1_hbm, kb1, 1, a, c).start()
    const_loads[1].start()

    for buf in (g1, g2, g3):
        @pl.when(jnp.logical_not(has_l))
        def _():
            buf[:, 0] = jnp.zeros((frames + 2, rows, chans), jnp.bfloat16)

        @pl.when(jnp.logical_not(has_r))
        def _():
            buf[:, cols + 1] = jnp.zeros((frames + 2, rows, chans), jnp.bfloat16)

        @pl.when(jnp.logical_not(has_f))
        def _():
            buf[pl.ds(frames, 2)] = jnp.zeros((2, cols + 2, rows, chans), jnp.bfloat16)

    barrier = pltpu.get_barrier_semaphore()
    for d in range(1, n):
        pl.semaphore_signal(
            barrier, inc=1, device_id={"tm": tm, "tile": lax.rem(me + d, n)}, device_id_type=MESH
        )
    for dt, ok_t in ((-1, has_p), (1, has_f)):
        for dw, ok_w in ((0, None), (-1, has_l), (1, has_r)):
            ok = ok_t if ok_w is None else jnp.logical_and(ok_t, ok_w)

            @pl.when(ok)
            def _():
                pl.semaphore_signal(
                    barrier, inc=1, device_id={"tm": tm + dt, "tile": me + dw}, device_id_type=MESH
                )

    def as_int(flag):
        return jnp.where(flag, 1, 0).astype(jnp.int32)

    peers = (n - 1) + (as_int(has_p) + as_int(has_f)) * (1 + as_int(has_l) + as_int(has_r))

    g1[pl.ds(0, frames), pl.ds(1, cols)] = g_ref[...]
    stats = []
    for x_ref in (x2_ref, x1_ref):
        for f in range(frames):
            x = x_ref[f].reshape(spot, chans).astype(f32)
            stats.append(jnp.sum(x, axis=0, keepdims=True))
            stats.append(jnp.sum(x * x, axis=0, keepdims=True))
    for i, row in enumerate(stats):
        mom[me, pl.ds(i, 1)] = row
    pl.semaphore_wait(barrier, peers)

    def halo(buf, stage):
        def copy(src, dst, slot, dt, dw):
            return pltpu.make_async_remote_copy(
                src_ref=src, dst_ref=dst,
                send_sem=halo_send.at[stage, slot], recv_sem=halo_recv.at[stage, slot],
                device_id={"tm": tm + dt, "tile": me + dw}, device_id_type=MESH,
            )

        own = pl.ds(0, frames)
        both = jnp.logical_and
        side = [
            (copy(buf.at[own, cols], buf.at[own, 0], 0, 0, 1), has_r, has_l),
            (copy(buf.at[own, 1], buf.at[own, cols + 1], 1, 0, -1), has_l, has_r),
        ]
        later = []
        for f in range(2):
            at = 2 + 3 * f
            mid = pl.ds(1, cols)
            later.append([
                (copy(buf.at[f, mid], buf.at[frames + f, mid], at, -1, 0), has_p, has_f),
                (copy(buf.at[f, cols], buf.at[frames + f, 0], at + 1, -1, 1),
                 both(has_p, has_r), both(has_f, has_l)),
                (copy(buf.at[f, 1], buf.at[frames + f, cols + 1], at + 2, -1, -1),
                 both(has_p, has_l), both(has_f, has_r)),
            ])
        return side, later

    def start(moves):
        for move, sends, _ in moves:
            pl.when(sends)(move.start)

    def arrive(moves):
        for move, _, receives in moves:
            pl.when(receives)(move.wait_recv)

    def sent(moves):
        for move, sends, _ in moves:
            pl.when(sends)(move.wait_send)

    def spread(buf, sends, recvs, index, source=None):
        out = []
        for d in range(1, n):
            to = lax.rem(me + d, n)
            src = buf.at[me] if source is None else source.at[to]
            out.append((
                pltpu.make_async_remote_copy(
                    src_ref=src, dst_ref=buf.at[me],
                    send_sem=sends.at[index, d], recv_sem=recvs.at[index, d],
                    device_id={"tm": tm, "tile": to}, device_id_type=MESH,
                ),
                pltpu.make_async_remote_copy(
                    src_ref=src, dst_ref=buf.at[lax.rem(me - d + n, n)],
                    send_sem=sends.at[index, d], recv_sem=recvs.at[index, d],
                    device_id={"tm": tm, "tile": to}, device_id_type=MESH,
                ),
            ))
        return out

    def total(buf):
        out = buf[0]
        for s in range(1, n):
            out = out + buf[s]
        return out

    halos = [halo(buf, i) for i, buf in enumerate((g1, g2, g3))]
    side, later = halos[0]
    mom_moves = spread(mom, st_send, st_recv, 0)
    start(side)
    for move, _ in mom_moves:
        move.start()
    start(later[0])
    start(later[1])

    row_of = lax.broadcasted_iota(jnp.int32, (cols, rows, chans), 1).reshape(spot, chans)
    not_last, not_first = row_of < rows - 1, row_of > 0

    def conv(buf, kb, k_hbm, which, halo_parts):
        side, later = halo_parts
        for step, a in enumerate((2, 1, 0)):
            arrive(side if step == 0 else later[step - 1])
            for c in range(3):
                load(k_hbm, kb, which, a, c).wait()

            def one(b, carry):
                left = jnp.concatenate(
                    [buf[2 - a : 2 - a + frames, 2 - c : 2 - c + cols].reshape(area, chans) for c in range(3)],
                    axis=1,
                )
                part = lax.dot_general(left, kb[3 * a + b], NT, preferred_element_type=f32)
                if step == 0:
                    acc[b] = part
                else:
                    acc[b] = acc[b] + part
                return carry

            lax.fori_loop(0, 3, one, 0)

    def section(x_ref, k, tot, gain, shift, buf, nxt, kb, k_hbm, halo_parts, sums, index, next_halo):
        inv = []
        for f in range(frames):
            at = 2 * frames * k + 2 * f
            mean = tot[at : at + 1] / cells
            var = tot[at + 1 : at + 2] / cells - mean * mean
            r = lax.rsqrt(var + epsilon)
            inv.append(r)
            xhat = (x_ref[f].reshape(spot, chans).astype(f32) - mean) * r
            z = xhat * gain[...] + shift[...]
            sig = jax.nn.sigmoid(z)
            xhat_s[f] = xhat
            coef_s[f] = sig * (1.0 + z * (1.0 - sig)) * gain[...]
        conv(buf, kb, k_hbm, k, halo_parts)
        for f in range(frames):
            at = pl.ds(f * spot, spot)
            up = jnp.where(not_last, pltpu.roll(acc[0, at], spot - 1, 0), 0.0)
            down = jnp.where(not_first, pltpu.roll(acc[2, at], 1, 0), 0.0)
            q = (up + acc[1, at] + down) * coef_s[f]
            q_s[f] = q
            sums[me, pl.ds(2 * f, 1)] = jnp.sum(q, axis=0, keepdims=True)
            sums[me, pl.ds(2 * f + 1, 1)] = jnp.sum(q * xhat_s[f], axis=0, keepdims=True)
        moves = spread(sums, st_send, st_recv, index)
        for move, _ in moves:
            move.start()
        for _, move in moves:
            move.wait_recv()
        means = times_exact(total(sums), group_m[...]) / cells
        for f in range(frames):
            m1, m2 = means[2 * f : 2 * f + 1], means[2 * f + 1 : 2 * f + 2]
            own = buf[f, 1 : 1 + cols].reshape(spot, chans).astype(f32)
            dx = own + inv[f] * (q_s[f] - m1 - xhat_s[f] * m2)
            nxt[f, 1 : 1 + cols] = dx.astype(jnp.bfloat16).reshape(cols, rows, chans)
            if f == 0:
                start(next_halo[1][0])
        start(next_halo[0])
        start(next_halo[1][1])
        return moves

    for _, move in mom_moves:
        move.wait_recv()
    const_loads[0].wait()
    tot = times_exact(total(mom), group_m[...])
    moves2 = section(x2_ref, 0, tot, gain2, shift2, g1, g2, kb2, k2_hbm, halos[0], sums2, 1, halos[1])
    moves1 = section(x1_ref, 1, tot, gain1, shift1, g2, g3, kb1, k1_hbm, halos[1], sums1, 2, halos[2])

    side, later = halos[2]
    result = None
    for step, a in enumerate((2, 1, 0)):
        arrive(side if step == 0 else later[step - 1])
        weights = jnp.concatenate(
            [jnp.concatenate([lat_ref[9 * a + 3 * b + c] for c in range(3)], axis=1) for b in range(3)],
            axis=0,
        )
        pixels = jnp.concatenate(
            [g3[2 - a : 2 - a + frames, 2 - c : 2 - c + cols].reshape(area, chans) for c in range(3)],
            axis=1,
        )
        part = lax.dot_general(weights, pixels, NT, preferred_element_type=f32)
        result = part if result is None else result + part
    lane = lax.broadcasted_iota(jnp.int32, (lat, area), 1)
    lane_row = lax.rem(lane, rows)
    up = jnp.where(lane_row < rows - 1, pltpu.roll(result[:lat], area - 1, 1), 0.0)
    down = jnp.where(lane_row > 0, pltpu.roll(result[2 * lat :], 1, 1), 0.0)
    pixel = up + result[lat : 2 * lat] + down
    const_loads[1].wait()
    placed = times_exact(pixel, place_m[...])
    for j in range(n):
        outgoing[j] = placed[:, j * area : (j + 1) * area]
    last = spread(incoming, a_send, a_recv, 0, outgoing)
    for move, _ in last:
        move.start()
    incoming[me] = outgoing[me]
    for _, move in last:
        move.wait_recv()
    answer = incoming[0]
    for s in range(1, n):
        answer = answer + pltpu.roll(incoming[s], s * (cols // 2), 1)
    out_ref[...] = answer

    for side, later in halos:
        sent(side)
        sent(later[0])
        sent(later[1])
    for moves in (mom_moves, moves2, moves1, last):
        for move, _ in moves:
            move.wait_send()


def shards(
    n_tm, n,
    first_input, second_input, output_grad,
    first_gain, first_shift, first_kernel,
    second_gain, second_shift, second_kernel,
    latent_kernel,
):
    frames, rows, cols, chans = first_input.shape
    lat = latent_kernel.shape[1]
    area = frames * rows * cols
    group_of = np.arange(chans) // (chans // GROUPS)
    group = (group_of[:, None] == group_of[None]).astype(ml_dtypes.bfloat16)
    per = frames * (rows // 2) // n
    tokens = area // 4
    f, w, h = np.meshgrid(np.arange(frames), np.arange(cols), np.arange(rows), indexing="ij")
    line = f * (rows // 2) + h // 2
    target = (line // per) * area + (2 * (h % 2) + w % 2) * tokens + (line % per) * (n * cols // 2) + w // 2
    place = (target.reshape(-1, 1) == np.arange(n * area)[None]).astype(ml_dtypes.bfloat16)

    def turned(value):
        return jnp.transpose(value, (0, 2, 1, 3))

    bf16, f32 = jnp.bfloat16, jnp.float32
    vmem = pl.BlockSpec(memory_space=pltpu.VMEM)
    anywhere = pl.BlockSpec(memory_space=pl.ANY)
    grid_buf = pltpu.VMEM((frames + 2, cols + 2, rows, chans), bf16)
    kernel_buf = pltpu.VMEM((9, chans, 3 * chans), bf16)
    plane = pltpu.VMEM((frames, cols * rows, chans), f32)
    stat = -(-4 * frames // 8) * 8
    dma = pltpu.SemaphoreType.DMA
    out = pl.pallas_call(
        functools.partial(body, n_tm, n),
        out_shape=jax.ShapeDtypeStruct((lat, area), f32),
        in_specs=[vmem] * 8 + [anywhere] * 4,
        out_specs=vmem,
        scratch_shapes=[
            grid_buf, grid_buf, grid_buf, kernel_buf, kernel_buf,
            pltpu.VMEM((chans, chans), bf16),
            pltpu.VMEM((area, n * area), bf16),
            pltpu.VMEM((3, area, chans), f32),
            plane, plane, plane,
            pltpu.VMEM((n, stat, chans), f32),
            pltpu.VMEM((n, 2 * frames, chans), f32),
            pltpu.VMEM((n, 2 * frames, chans), f32),
            pltpu.VMEM((n, lat, area), f32),
            pltpu.VMEM((n, lat, area), f32),
            dma((2, 3, 3)), dma((2,)), dma((3, 8)), dma((3, 8)),
            dma((3, n)), dma((3, n)), dma((1, n)), dma((1, n)),
        ],
        compiler_params=pltpu.CompilerParams(
            collective_id=0, has_side_effects=True, vmem_limit_bytes=56 * 1024 * 1024
        ),
        cost_estimate=pl.CostEstimate(
            flops=4 * area * 27 * chans * chans, bytes_accessed=4 * 27 * chans * chans, transcendentals=2 * area * chans
        ),
    )(
        turned(second_input), turned(first_input), turned(output_grad),
        second_gain.reshape(1, -1), second_shift.reshape(1, -1),
        first_gain.reshape(1, -1), first_shift.reshape(1, -1),
        latent_kernel,
        second_kernel.reshape(9, 3, chans, chans), first_kernel.reshape(9, 3, chans, chans),
        jnp.asarray(group), jnp.asarray(place),
    )
    return out.reshape(4 * lat, tokens)


def solution(mesh):
    cells = P("tm", None, "tile", None)
    return jax.shard_map(
        functools.partial(shards, mesh.shape["tm"], mesh.shape["tile"]),
        mesh=mesh,
        in_specs=(cells,) * 3 + (P(),) * 7,
        out_specs=P(None, ("tm", "tile")),
        check_vma=False,
    )
```

profile of v0, /device:TPU:0, one launch (start us, length us, event | category | flops | bytes accessed | tf_op | source)
XLA Modules:
  0.0 58.8 jit_solution(10171892479080088916)
XLA Ops:
  0.0 1.3 %reshape.23.gain1 = f32[1,384]{1,0:T(1,128)} reshape(f32[384]{0:T(512)} %param.15) | data formatting | bytes 3072 | tf_op jit(solution)/shard_map/reshape | solution.py:360
  1.3 1.2 %reshape.24.shift1 = f32[1,384]{1,0:T(1,128)} reshape(f32[384]{0:T(512)} %param.16) | data formatting | bytes 3072 | tf_op jit(solution)/shard_map/reshape | solution.py:360
  2.5 1.2 %reshape.21.gain2 = f32[1,384]{1,0:T(1,128)} reshape(f32[384]{0:T(512)} %param.18) | data formatting | bytes 3072 | tf_op jit(solution)/shard_map/reshape | solution.py:359
  3.7 1.3 %reshape.22.shift2 = f32[1,384]{1,0:T(1,128)} reshape(f32[384]{0:T(512)} %param.19) | data formatting | bytes 3072 | tf_op jit(solution)/shard_map/reshape | solution.py:359
  5.0 1.6 %copy.19 = bf16[2,32,4,384]{3,1,2,0:T(8,128)(2,1)} copy(bf16[2,32,4,384]{3,2,1,0:T(4,128)(2,1)} %param.13) | data formatting | bytes 393216 | tf_op args[1]
  6.6 1.8 %copy_bitcast_fusion = (bf16[2,4,32,384]{3,2,1,0:T(8,128)(2,1)}, bf16[2,4,32,384]{3,2,1,0:T(8,128)(2,1)}) fusion(bf16[2,32,4,384]{3,2,1,0:T(4,128)(2,1)} %param.14, bf16[2,32,4,384]{3,2,1,0:T(4,128)(2,1)} %param.12), kind=kLoop, calls=%fused_computation | loop fusion | bytes 786432 | tf_op jit(solution)/shard_map/transpose | solution.py:322
  8.4 49.0 %shard_map.118 = f32[16,256]{1,0:T(8,128)} custom-call(bf16[2,4,32,384]{3,2,1,0:T(8,128)(2,1)} %bitcast.11, bf16[2,4,32,384]{3,2,1,0:T(8,128)(2,1)} %get-tuple-element.6.x1_ref, bf16[2,4,32,384]{3,2,1,0:T(8,128)(2,1)} %get-tuple-element.5.g_ref, f32[1,384]{1,0:T(1,128)} %reshape.21.gain2, f32[1,384]{1,0:T(1,128)} %reshape.22.shift2, ...), custom_call_target="tpu_custom_call" | custom-call | flops 4076863488 | bytes 15925248 | tf_op jit(solution)/shard_map/pallas_call | solution.py:332
  57.4 1.4 %reshape.27 = f32[64,64]{1,0:T(8,128)} reshape(f32[16,256]{1,0:T(8,128)} %shard_map.118) | data formatting | bytes 32768 | tf_op jit(solution)/shard_map/reshape | solution.py:365
where the time goes:
time: 59.2 us; the launch traced here: 58.8 us
  Pallas kernels  49 us (83%)
  local copies, waits for them, and re-layouts  9.84 us (17%)
    pallas_call x1, Pallas kernels, shards(): pl.pallas_call(functools.partial(body, n_tm, n), out_shape=jax.ShapeDtype...  49 us
    transpose x1, local copies, waits for them, and re-layouts, turned(): return jnp.transpose(value, (0, 2, 1, 3))  1.82 us
    unnamed x1, local copies, waits for them, and re-layouts  1.62 us
    reshape x1, local copies, waits for them, and re-layouts, shards(): return out.reshape(4 * lat, tokens)  1.4 us
    reshape x1, local copies, waits for them, and re-layouts, shards(): first_gain.reshape(1, -1)  1.27 us
    reshape x1, local copies, waits for them, and re-layouts, shards(): second_shift.reshape(1, -1)  1.26 us
    reshape x1, local copies, waits for them, and re-layouts, shards(): second_gain.reshape(1, -1)  1.24 us
    reshape x1, local copies, waits for them, and re-layouts, shards(): first_shift.reshape(1, -1)  1.22 us

commit v1 on v0

--- a/solution.py
+++ b/solution.py
@@ -31,16 +31,16 @@
 
 def body(
     n_tm, n,
-    x2_ref, x1_ref, g_ref, gain2, shift2, gain1, shift1, lat_ref,
-    k2_hbm, k1_hbm, group_hbm, place_hbm,
+    gain2, shift2, gain1, shift1, lat_ref,
+    g_hbm, x2_hbm, x1_hbm, k2_hbm, k1_hbm, group_hbm, place_hbm,
     out_ref,
-    g1, g2, g3, kb2, kb1, group_m, place_m, acc, xhat_s, coef_s, q_s,
+    raw, x_s, g1, g2, g3, kb2, kb1, group_m, place_m, acc, xhat_s, coef_s, q_s,
     mom, sums2, sums1, outgoing, incoming,
     k_sem, c_sem, halo_send, halo_recv, st_send, st_recv, a_send, a_recv,
 ):
     tm = lax.axis_index("tm")
     me = lax.axis_index("tile")
-    frames, cols, rows, chans = x2_ref.shape
+    frames, rows, cols, chans = g_hbm.shape
     lat = lat_ref.shape[1]
     spot = cols * rows
     area = frames * spot
@@ -60,6 +60,12 @@
         pltpu.make_async_copy(group_hbm, group_m, c_sem.at[0]),
         pltpu.make_async_copy(place_hbm, place_m, c_sem.at[1]),
     ]
+    inputs = [
+        pltpu.make_async_copy(src, raw.at[i], c_sem.at[2 + i])
+        for i, src in enumerate((g_hbm, x2_hbm, x1_hbm))
+    ]
+    for copy in inputs:
+        copy.start()
     const_loads[0].start()
     for a in (2, 1, 0):
         for c in range(3):
@@ -102,15 +108,17 @@
 
     peers = (n - 1) + (as_int(has_p) + as_int(has_f)) * (1 + as_int(has_l) + as_int(has_r))
 
-    g1[pl.ds(0, frames), pl.ds(1, cols)] = g_ref[...]
-    stats = []
-    for x_ref in (x2_ref, x1_ref):
-        for f in range(frames):
-            x = x_ref[f].reshape(spot, chans).astype(f32)
-            stats.append(jnp.sum(x, axis=0, keepdims=True))
-            stats.append(jnp.sum(x * x, axis=0, keepdims=True))
-    for i, row in enumerate(stats):
-        mom[me, pl.ds(i, 1)] = row
+    to_w = lax.broadcasted_iota(jnp.int32, (cols, rows, spot), 0)
+    to_h = lax.broadcasted_iota(jnp.int32, (cols, rows, spot), 1)
+    source = lax.broadcasted_iota(jnp.int32, (cols, rows, spot), 2)
+    turn = jnp.where(source == to_h * cols + to_w, 1.0, 0.0).reshape(spot, spot).astype(jnp.bfloat16)
+
+    def turned(i, f):
+        return jnp.dot(turn, raw[i, f].reshape(spot, chans), preferred_element_type=f32)
+
+    inputs[0].wait()
+    for f in range(frames):
+        g1[f, 1 : 1 + cols] = turned(0, f).astype(jnp.bfloat16).reshape(cols, rows, chans)
     pl.semaphore_wait(barrier, peers)
 
     def halo(buf, stage):
@@ -179,15 +187,24 @@
 
     halos = [halo(buf, i) for i, buf in enumerate((g1, g2, g3))]
     side, later = halos[0]
+    start(side)
+    start(later[0])
+    start(later[1])
+
+    for k in range(2):
+        inputs[1 + k].wait()
+        for f in range(frames):
+            x = turned(1 + k, f)
+            x_s[k, f] = x
+            at = 2 * frames * k + 2 * f
+            mom[me, pl.ds(at, 1)] = jnp.sum(x, axis=0, keepdims=True)
+            mom[me, pl.ds(at + 1, 1)] = jnp.sum(x * x, axis=0, keepdims=True)
     mom_moves = spread(mom, st_send, st_recv, 0)
-    start(side)
     for move, _ in mom_moves:
         move.start()
-    start(later[0])
-    start(later[1])
-
-    row_of = lax.broadcasted_iota(jnp.int32, (cols, rows, chans), 1).reshape(spot, chans)
-    not_last, not_first = row_of < rows - 1, row_of > 0
+
+    lane_h = lax.rem(lax.broadcasted_iota(jnp.int32, (chans, spot), 1), rows)
+    not_last, not_first = lane_h < rows - 1, lane_h > 0
 
     def conv(buf, kb, k_hbm, which, halo_parts):
         side, later = halo_parts
@@ -196,21 +213,15 @@
             for c in range(3):
                 load(k_hbm, kb, which, a, c).wait()
 
-            def one(b, carry):
-                left = jnp.concatenate(
-                    [buf[2 - a : 2 - a + frames, 2 - c : 2 - c + cols].reshape(area, chans) for c in range(3)],
-                    axis=1,
-                )
-                part = lax.dot_general(left, kb[3 * a + b], NT, preferred_element_type=f32)
-                if step == 0:
-                    acc[b] = part
-                else:
-                    acc[b] = acc[b] + part
-                return carry
-
-            lax.fori_loop(0, 3, one, 0)
-
-    def section(x_ref, k, tot, gain, shift, buf, nxt, kb, k_hbm, halo_parts, sums, index, next_halo):
+            pixels = jnp.concatenate(
+                [buf[2 - a : 2 - a + frames, 2 - c : 2 - c + cols].reshape(area, chans) for c in range(3)],
+                axis=1,
+            )
+            weights = kb[3 * a : 3 * a + 3].reshape(3 * chans, 3 * chans)
+            part = lax.dot_general(weights, pixels, NT, preferred_element_type=f32)
+            acc[...] = part if step == 0 else acc[...] + part
+
+    def section(k, tot, gain, shift, buf, nxt, kb, k_hbm, halo_parts, sums, index, next_halo):
         inv = []
         for f in range(frames):
             at = 2 * frames * k + 2 * f
@@ -218,17 +229,17 @@
             var = tot[at + 1 : at + 2] / cells - mean * mean
             r = lax.rsqrt(var + epsilon)
             inv.append(r)
-            xhat = (x_ref[f].reshape(spot, chans).astype(f32) - mean) * r
-            z = xhat * gain[...] + shift[...]
+            xhat = (x_s[k, f] - mean) * r
+            z = xhat * gain + shift
             sig = jax.nn.sigmoid(z)
             xhat_s[f] = xhat
-            coef_s[f] = sig * (1.0 + z * (1.0 - sig)) * gain[...]
+            coef_s[f] = sig * (1.0 + z * (1.0 - sig)) * gain
         conv(buf, kb, k_hbm, k, halo_parts)
         for f in range(frames):
             at = pl.ds(f * spot, spot)
-            up = jnp.where(not_last, pltpu.roll(acc[0, at], spot - 1, 0), 0.0)
-            down = jnp.where(not_first, pltpu.roll(acc[2, at], 1, 0), 0.0)
-            q = (up + acc[1, at] + down) * coef_s[f]
+            up = jnp.where(not_last, pltpu.roll(acc[:chans, at], spot - 1, 1), 0.0)
+            down = jnp.where(not_first, pltpu.roll(acc[2 * chans :, at], 1, 1), 0.0)
+            q = (up + acc[chans : 2 * chans, at] + down).T * coef_s[f]
             q_s[f] = q
             sums[me, pl.ds(2 * f, 1)] = jnp.sum(q, axis=0, keepdims=True)
             sums[me, pl.ds(2 * f + 1, 1)] = jnp.sum(q * xhat_s[f], axis=0, keepdims=True)
@@ -253,8 +264,12 @@
         move.wait_recv()
     const_loads[0].wait()
     tot = times_exact(total(mom), group_m[...])
-    moves2 = section(x2_ref, 0, tot, gain2, shift2, g1, g2, kb2, k2_hbm, halos[0], sums2, 1, halos[1])
-    moves1 = section(x1_ref, 1, tot, gain1, shift1, g2, g3, kb1, k1_hbm, halos[1], sums1, 2, halos[2])
+
+    def as_row(ref):
+        return ref[...].reshape(1, chans)
+
+    moves2 = section(0, tot, as_row(gain2), as_row(shift2), g1, g2, kb2, k2_hbm, halos[0], sums2, 1, halos[1])
+    moves1 = section(1, tot, as_row(gain1), as_row(shift1), g2, g3, kb1, k1_hbm, halos[1], sums1, 2, halos[2])
 
     side, later = halos[2]
     result = None
@@ -318,9 +333,6 @@
     target = (line // per) * area + (2 * (h % 2) + w % 2) * tokens + (line % per) * (n * cols // 2) + w // 2
     place = (target.reshape(-1, 1) == np.arange(n * area)[None]).astype(ml_dtypes.bfloat16)
 
-    def turned(value):
-        return jnp.transpose(value, (0, 2, 1, 3))
-
     bf16, f32 = jnp.bfloat16, jnp.float32
     vmem = pl.BlockSpec(memory_space=pltpu.VMEM)
     anywhere = pl.BlockSpec(memory_space=pl.ANY)
@@ -332,20 +344,22 @@
     out = pl.pallas_call(
         functools.partial(body, n_tm, n),
         out_shape=jax.ShapeDtypeStruct((lat, area), f32),
-        in_specs=[vmem] * 8 + [anywhere] * 4,
+        in_specs=[vmem] * 5 + [anywhere] * 7,
         out_specs=vmem,
         scratch_shapes=[
+            pltpu.VMEM((3, frames, rows, cols, chans), bf16),
+            pltpu.VMEM((2, frames, rows * cols, chans), f32),
             grid_buf, grid_buf, grid_buf, kernel_buf, kernel_buf,
             pltpu.VMEM((chans, chans), bf16),
             pltpu.VMEM((area, n * area), bf16),
-            pltpu.VMEM((3, area, chans), f32),
+            pltpu.VMEM((3 * chans, area), f32),
             plane, plane, plane,
             pltpu.VMEM((n, stat, chans), f32),
             pltpu.VMEM((n, 2 * frames, chans), f32),
             pltpu.VMEM((n, 2 * frames, chans), f32),
             pltpu.VMEM((n, lat, area), f32),
             pltpu.VMEM((n, lat, area), f32),
-            dma((2, 3, 3)), dma((2,)), dma((3, 8)), dma((3, 8)),
+            dma((2, 3, 3)), dma((5,)), dma((3, 8)), dma((3, 8)),
             dma((3, n)), dma((3, n)), dma((1, n)), dma((1, n)),
         ],
         compiler_params=pltpu.CompilerParams(
@@ -355,10 +369,8 @@
             flops=4 * area * 27 * chans * chans, bytes_accessed=4 * 27 * chans * chans, transcendentals=2 * area * chans
         ),
     )(
-        turned(second_input), turned(first_input), turned(output_grad),
-        second_gain.reshape(1, -1), second_shift.reshape(1, -1),
-        first_gain.reshape(1, -1), first_shift.reshape(1, -1),
-        latent_kernel,
+        second_gain, second_shift, first_gain, first_shift, latent_kernel,
+        output_grad, second_input, first_input,
         second_kernel.reshape(9, 3, chans, chans), first_kernel.reshape(9, 3, chans, chans),
         jnp.asarray(group), jnp.asarray(place),
     )

time: 59.2 us -> 51.9 us (0.88)
  local copies, waits for them, and re-layouts: 9.84 us -> 1.4 us
  Pallas kernels: 49 us -> 50.3 us
    reshape x4 -> x0, local copies, waits for them, and re-layouts: 5 us -> none  [the longest x1 1.27 us: shards(): first_gain.reshape(1, -1)]
    transpose x1 -> x0, local copies, waits for them, and re-layouts: 1.82 us -> none  [turned(): return jnp.transpose(value, (0, 2, 1, 3))]
    unnamed x1 -> x0, local copies, waits for them, and re-layouts: 1.62 us -> none
    pallas_call x1, Pallas kernels: 49 us -> 50.3 us  [shards(): pl.pallas_call(functools.partial(body, n_tm, n), out_shape=jax.ShapeDtype...]
where the time goes in v1:
time: 51.9 us; the launch traced here: 51.7 us
  Pallas kernels  50.3 us (97%)
  local copies, waits for them, and re-layouts  1.4 us (3%)
    pallas_call x1, Pallas kernels, shards(): pl.pallas_call(functools.partial(body, n_tm, n), out_shape=jax.ShapeDtype...  50.3 us
    reshape x1, local copies, waits for them, and re-layouts, shards(): return out.reshape(4 * lat, tokens)  1.4 us

profile of v1, /device:TPU:0, one launch (start us, length us, event | category | flops | bytes accessed | tf_op | source)
XLA Modules:
  0.0 51.7 jit_solution(7175455571806061866)
XLA Ops:
  0.0 50.3 %shard_map.118 = f32[16,256]{1,0:T(8,128)} custom-call(f32[384]{0:T(512)} %gain2.1, f32[384]{0:T(512)} %shift2.1, f32[384]{0:T(512)} %gain1.1, f32[384]{0:T(512)} %shift1.1, bf16[27,16,384]{2,1,0:T(8,128)(2,1)} %lat_ref.1, bf16[2,32,4,384]{3,2,1,0:T(4,128)(2,1)} %g_hbm.1, bf16[2,32,4,384]{3,2,1,0:T(4,128)(2,1)} %x2_hbm.1, bf16[2,32,4,384]{3,2,1,0:T(4,128)(2,1)} %x1_hbm.1, ...), custom_call_target="tpu_custom_call" | custom-call | flops 4076863488 | bytes 15925248 | tf_op jit(solution)/shard_map/pallas_call | solution.py:344
  50.3 1.4 %reshape.11 = f32[64,64]{1,0:T(8,128)} reshape(f32[16,256]{1,0:T(8,128)} %shard_map.118) | data formatting | bytes 32768 | tf_op jit(solution)/shard_map/reshape | solution.py:377

commit v2 on v1

--- a/solution.py
+++ b/solution.py
@@ -35,7 +35,7 @@
     g_hbm, x2_hbm, x1_hbm, k2_hbm, k1_hbm, group_hbm, place_hbm,
     out_ref,
     raw, x_s, g1, g2, g3, kb2, kb1, group_m, place_m, acc, xhat_s, coef_s, q_s,
-    mom, sums2, sums1, outgoing, incoming,
+    mom, mom_all, sums2, sums1, outgoing, incoming,
     k_sem, c_sem, halo_send, halo_recv, st_send, st_recv, a_send, a_recv,
 ):
     tm = lax.axis_index("tm")
@@ -93,20 +93,17 @@
         pl.semaphore_signal(
             barrier, inc=1, device_id={"tm": tm, "tile": lax.rem(me + d, n)}, device_id_type=MESH
         )
-    for dt, ok_t in ((-1, has_p), (1, has_f)):
-        for dw, ok_w in ((0, None), (-1, has_l), (1, has_r)):
-            ok = ok_t if ok_w is None else jnp.logical_and(ok_t, ok_w)
-
-            @pl.when(ok)
-            def _():
-                pl.semaphore_signal(
-                    barrier, inc=1, device_id={"tm": tm + dt, "tile": me + dw}, device_id_type=MESH
-                )
+    for dt, ok in ((-1, has_p), (1, has_f)):
+        @pl.when(ok)
+        def _():
+            pl.semaphore_signal(
+                barrier, inc=1, device_id={"tm": tm + dt, "tile": me}, device_id_type=MESH
+            )
 
     def as_int(flag):
         return jnp.where(flag, 1, 0).astype(jnp.int32)
 
-    peers = (n - 1) + (as_int(has_p) + as_int(has_f)) * (1 + as_int(has_l) + as_int(has_r))
+    peers = (n - 1) + as_int(has_p) + as_int(has_f)
 
     to_w = lax.broadcasted_iota(jnp.int32, (cols, rows, spot), 0)
     to_h = lax.broadcasted_iota(jnp.int32, (cols, rows, spot), 1)
@@ -119,6 +116,14 @@
     inputs[0].wait()
     for f in range(frames):
         g1[f, 1 : 1 + cols] = turned(0, f).astype(jnp.bfloat16).reshape(cols, rows, chans)
+    for k in range(2):
+        inputs[1 + k].wait()
+        for f in range(frames):
+            x = turned(1 + k, f)
+            x_s[k, f] = x
+            at = 2 * frames * k + 2 * f
+            mom[me, pl.ds(at, 1)] = jnp.sum(x, axis=0, keepdims=True)
+            mom[me, pl.ds(at + 1, 1)] = jnp.sum(x * x, axis=0, keepdims=True)
     pl.semaphore_wait(barrier, peers)
 
     def halo(buf, stage):
@@ -129,24 +134,28 @@
                 device_id={"tm": tm + dt, "tile": me + dw}, device_id_type=MESH,
             )
 
-        own = pl.ds(0, frames)
+        own, next_two, first_two = pl.ds(0, frames), pl.ds(frames, 2), pl.ds(0, 2)
+        inner = pl.ds(2, cols - 2)
         both = jnp.logical_and
         side = [
             (copy(buf.at[own, cols], buf.at[own, 0], 0, 0, 1), has_r, has_l),
             (copy(buf.at[own, 1], buf.at[own, cols + 1], 1, 0, -1), has_l, has_r),
         ]
-        later = []
-        for f in range(2):
-            at = 2 + 3 * f
-            mid = pl.ds(1, cols)
-            later.append([
-                (copy(buf.at[f, mid], buf.at[frames + f, mid], at, -1, 0), has_p, has_f),
-                (copy(buf.at[f, cols], buf.at[frames + f, 0], at + 1, -1, 1),
-                 both(has_p, has_r), both(has_f, has_l)),
-                (copy(buf.at[f, 1], buf.at[frames + f, cols + 1], at + 2, -1, -1),
-                 both(has_p, has_l), both(has_f, has_r)),
-            ])
-        return side, later
+        edges = [
+            (copy(buf.at[first_two, col], buf.at[next_two, col], slot, -1, 0), has_p, has_f)
+            for slot, col in ((2, 1), (3, cols))
+        ]
+        inners = [
+            [(copy(buf.at[f, inner], buf.at[frames + f, inner], 4 + f, -1, 0), has_p, has_f)]
+            for f in range(2)
+        ]
+        passed = [
+            (copy(buf.at[next_two, cols], buf.at[next_two, 0], 6, 0, 1),
+             both(has_f, has_r), both(has_f, has_l)),
+            (copy(buf.at[next_two, 1], buf.at[next_two, cols + 1], 7, 0, -1),
+             both(has_f, has_l), both(has_f, has_r)),
+        ]
+        return side, edges, inners, passed
 
     def start(moves):
         for move, sends, _ in moves:
@@ -186,33 +195,42 @@
         return out
 
     halos = [halo(buf, i) for i, buf in enumerate((g1, g2, g3))]
-    side, later = halos[0]
-    start(side)
-    start(later[0])
-    start(later[1])
-
-    for k in range(2):
-        inputs[1 + k].wait()
-        for f in range(frames):
-            x = turned(1 + k, f)
-            x_s[k, f] = x
-            at = 2 * frames * k + 2 * f
-            mom[me, pl.ds(at, 1)] = jnp.sum(x, axis=0, keepdims=True)
-            mom[me, pl.ds(at + 1, 1)] = jnp.sum(x * x, axis=0, keepdims=True)
+    def send_own(moves):
+        start(moves[0])
+        start(moves[1])
+        for part in moves[2]:
+            start(part)
+
     mom_moves = spread(mom, st_send, st_recv, 0)
+    start(halos[0][0])
     for move, _ in mom_moves:
         move.start()
+    start(halos[0][1])
+    for part in halos[0][2]:
+        start(part)
 
     lane_h = lax.rem(lax.broadcasted_iota(jnp.int32, (chans, spot), 1), rows)
     not_last, not_first = lane_h < rows - 1, lane_h > 0
 
-    def conv(buf, kb, k_hbm, which, halo_parts):
-        side, later = halo_parts
+    def frames_ready(moves, step):
+        side, edges, inners, passed = moves
+        if step == 0:
+            arrive(side)
+        elif step == 1:
+            arrive(inners[0])
+            arrive(passed)
+        else:
+            arrive(inners[1])
+
+    def pass_on(moves):
+        arrive(moves[1])
+        start(moves[3])
+
+    def conv(buf, kb, k_hbm, which, moves, between):
         for step, a in enumerate((2, 1, 0)):
-            arrive(side if step == 0 else later[step - 1])
+            frames_ready(moves, step)
             for c in range(3):
                 load(k_hbm, kb, which, a, c).wait()
-
             pixels = jnp.concatenate(
                 [buf[2 - a : 2 - a + frames, 2 - c : 2 - c + cols].reshape(area, chans) for c in range(3)],
                 axis=1,
@@ -220,21 +238,32 @@
             weights = kb[3 * a : 3 * a + 3].reshape(3 * chans, 3 * chans)
             part = lax.dot_general(weights, pixels, NT, preferred_element_type=f32)
             acc[...] = part if step == 0 else acc[...] + part
-
-    def section(k, tot, gain, shift, buf, nxt, kb, k_hbm, halo_parts, sums, index, next_halo):
+            if step == 0:
+                pass_on(moves)
+                between()
+
+    def section(k, gain, shift, buf, nxt, kb, k_hbm, moves, sums, index, next_moves):
         inv = []
-        for f in range(frames):
-            at = 2 * frames * k + 2 * f
-            mean = tot[at : at + 1] / cells
-            var = tot[at + 1 : at + 2] / cells - mean * mean
-            r = lax.rsqrt(var + epsilon)
-            inv.append(r)
-            xhat = (x_s[k, f] - mean) * r
-            z = xhat * gain + shift
-            sig = jax.nn.sigmoid(z)
-            xhat_s[f] = xhat
-            coef_s[f] = sig * (1.0 + z * (1.0 - sig)) * gain
-        conv(buf, kb, k_hbm, k, halo_parts)
+
+        def factors():
+            if k == 0:
+                for _, move in mom_moves:
+                    move.wait_recv()
+                const_loads[0].wait()
+                mom_all[...] = times_exact(total(mom), group_m[...])
+            for f in range(frames):
+                at = 2 * frames * k + 2 * f
+                mean = mom_all[at : at + 1] / cells
+                var = mom_all[at + 1 : at + 2] / cells - mean * mean
+                r = lax.rsqrt(var + epsilon)
+                inv.append(r)
+                xhat = (x_s[k, f] - mean) * r
+                z = xhat * gain + shift
+                sig = jax.nn.sigmoid(z)
+                xhat_s[f] = xhat
+                coef_s[f] = sig * (1.0 + z * (1.0 - sig)) * gain
+
+        conv(buf, kb, k_hbm, k, moves, factors)
         for f in range(frames):
             at = pl.ds(f * spot, spot)
             up = jnp.where(not_last, pltpu.roll(acc[:chans, at], spot - 1, 1), 0.0)
@@ -243,10 +272,10 @@
             q_s[f] = q
             sums[me, pl.ds(2 * f, 1)] = jnp.sum(q, axis=0, keepdims=True)
             sums[me, pl.ds(2 * f + 1, 1)] = jnp.sum(q * xhat_s[f], axis=0, keepdims=True)
-        moves = spread(sums, st_send, st_recv, index)
-        for move, _ in moves:
+        sum_moves = spread(sums, st_send, st_recv, index)
+        for move, _ in sum_moves:
             move.start()
-        for _, move in moves:
+        for _, move in sum_moves:
             move.wait_recv()
         means = times_exact(total(sums), group_m[...]) / cells
         for f in range(frames):
@@ -254,27 +283,18 @@
             own = buf[f, 1 : 1 + cols].reshape(spot, chans).astype(f32)
             dx = own + inv[f] * (q_s[f] - m1 - xhat_s[f] * m2)
             nxt[f, 1 : 1 + cols] = dx.astype(jnp.bfloat16).reshape(cols, rows, chans)
-            if f == 0:
-                start(next_halo[1][0])
-        start(next_halo[0])
-        start(next_halo[1][1])
-        return moves
-
-    for _, move in mom_moves:
-        move.wait_recv()
-    const_loads[0].wait()
-    tot = times_exact(total(mom), group_m[...])
+        send_own(next_moves)
+        return sum_moves
 
     def as_row(ref):
         return ref[...].reshape(1, chans)
 
-    moves2 = section(0, tot, as_row(gain2), as_row(shift2), g1, g2, kb2, k2_hbm, halos[0], sums2, 1, halos[1])
-    moves1 = section(1, tot, as_row(gain1), as_row(shift1), g2, g3, kb1, k1_hbm, halos[1], sums1, 2, halos[2])
-
-    side, later = halos[2]
+    moves2 = section(0, as_row(gain2), as_row(shift2), g1, g2, kb2, k2_hbm, halos[0], sums2, 1, halos[1])
+    moves1 = section(1, as_row(gain1), as_row(shift1), g2, g3, kb1, k1_hbm, halos[1], sums1, 2, halos[2])
+
     result = None
     for step, a in enumerate((2, 1, 0)):
-        arrive(side if step == 0 else later[step - 1])
+        frames_ready(halos[2], step)
         weights = jnp.concatenate(
             [jnp.concatenate([lat_ref[9 * a + 3 * b + c] for c in range(3)], axis=1) for b in range(3)],
             axis=0,
@@ -285,6 +305,8 @@
         )
         part = lax.dot_general(weights, pixels, NT, preferred_element_type=f32)
         result = part if result is None else result + part
+        if step == 0:
+            pass_on(halos[2])
     lane = lax.broadcasted_iota(jnp.int32, (lat, area), 1)
     lane_row = lax.rem(lane, rows)
     up = jnp.where(lane_row < rows - 1, pltpu.roll(result[:lat], area - 1, 1), 0.0)
@@ -305,10 +327,9 @@
         answer = answer + pltpu.roll(incoming[s], s * (cols // 2), 1)
     out_ref[...] = answer
 
-    for side, later in halos:
-        sent(side)
-        sent(later[0])
-        sent(later[1])
+    for side, edges, inners, passed in halos:
+        for part in (side, edges, inners[0], inners[1], passed):
+            sent(part)
     for moves in (mom_moves, moves2, moves1, last):
         for move, _ in moves:
             move.wait_send()
@@ -355,6 +376,7 @@
             pltpu.VMEM((3 * chans, area), f32),
             plane, plane, plane,
             pltpu.VMEM((n, stat, chans), f32),
+            pltpu.VMEM((stat, chans), f32),
             pltpu.VMEM((n, 2 * frames, chans), f32),
             pltpu.VMEM((n, 2 * frames, chans), f32),
             pltpu.VMEM((n, lat, area), f32),

time: 51.9 us -> 51.2 us (0.987)
  Pallas kernels: 50.3 us -> 49.6 us
    pallas_call x1, Pallas kernels: 50.3 us -> 49.6 us  [shards(): pl.pallas_call(functools.partial(body, n_tm, n), out_shape=jax.ShapeDtype...]
where the time goes in v2:
time: 51.2 us; the launch traced here: 51 us
  Pallas kernels  49.6 us (97%)
  local copies, waits for them, and re-layouts  1.4 us (3%)
    pallas_call x1, Pallas kernels, shards(): pl.pallas_call(functools.partial(body, n_tm, n), out_shape=jax.ShapeDtype...  49.6 us
    reshape x1, local copies, waits for them, and re-layouts, shards(): return out.reshape(4 * lat, tokens)  1.4 us

profile of v2, /device:TPU:0, one launch (start us, length us, event | category | flops | bytes accessed | tf_op | source)
XLA Modules:
  0.0 51.0 jit_solution(10814983343086811929)
XLA Ops:
  0.0 49.6 %shard_map.118 = f32[16,256]{1,0:T(8,128)} custom-call(f32[384]{0:T(512)} %gain2.1, f32[384]{0:T(512)} %shift2.1, f32[384]{0:T(512)} %gain1.1, f32[384]{0:T(512)} %shift1.1, bf16[27,16,384]{2,1,0:T(8,128)(2,1)} %lat_ref.1, bf16[2,32,4,384]{3,2,1,0:T(4,128)(2,1)} %g_hbm.1, bf16[2,32,4,384]{3,2,1,0:T(4,128)(2,1)} %x2_hbm.1, bf16[2,32,4,384]{3,2,1,0:T(4,128)(2,1)} %x1_hbm.1, ...), custom_call_target="tpu_custom_call" | custom-call | flops 4076863488 | bytes 15925248 | tf_op jit(solution)/shard_map/pallas_call | solution.py:365
  49.6 1.4 %reshape.11 = f32[64,64]{1,0:T(8,128)} reshape(f32[16,256]{1,0:T(8,128)} %shard_map.118) | data formatting | bytes 32768 | tf_op jit(solution)/shard_map/reshape | solution.py:399

commit v3 on v2

--- a/solution.py
+++ b/solution.py
@@ -67,13 +67,8 @@
     for copy in inputs:
         copy.start()
     const_loads[0].start()
-    for a in (2, 1, 0):
-        for c in range(3):
-            load(k2_hbm, kb2, 0, a, c).start()
-    for a in (2, 1, 0):
-        for c in range(3):
-            load(k1_hbm, kb1, 1, a, c).start()
-    const_loads[1].start()
+    for c in range(3):
+        load(k2_hbm, kb2, 0, 2, c).start()
 
     for buf in (g1, g2, g3):
         @pl.when(jnp.logical_not(has_l))
@@ -208,6 +203,9 @@
     start(halos[0][1])
     for part in halos[0][2]:
         start(part)
+    for a in (1, 0):
+        for c in range(3):
+            load(k2_hbm, kb2, 0, a, c).start()
 
     lane_h = lax.rem(lax.broadcasted_iota(jnp.int32, (chans, spot), 1), rows)
     not_last, not_first = lane_h < rows - 1, lane_h > 0
@@ -249,6 +247,10 @@
             if k == 0:
                 for _, move in mom_moves:
                     move.wait_recv()
+                for a in (2, 1, 0):
+                    for c in range(3):
+                        load(k1_hbm, kb1, 1, a, c).start()
+                const_loads[1].start()
                 const_loads[0].wait()
                 mom_all[...] = times_exact(total(mom), group_m[...])
             for f in range(frames):
@@ -314,18 +316,23 @@
     pixel = up + result[lat : 2 * lat] + down
     const_loads[1].wait()
     placed = times_exact(pixel, place_m[...])
+    half = area // 2
     for j in range(n):
-        outgoing[j] = placed[:, j * area : (j + 1) * area]
+        outgoing[j] = placed[:, j * half : (j + 1) * half]
     last = spread(incoming, a_send, a_recv, 0, outgoing)
     for move, _ in last:
         move.start()
     incoming[me] = outgoing[me]
     for _, move in last:
         move.wait_recv()
-    answer = incoming[0]
-    for s in range(1, n):
-        answer = answer + pltpu.roll(incoming[s], s * (cols // 2), 1)
-    out_ref[...] = answer
+    width = n * cols // 2
+    low = lax.rem(lax.broadcasted_iota(jnp.int32, (lat, half), 1), width) < width // 2
+    lower = upper = jnp.zeros((lat, half), f32)
+    for s in range(n):
+        got = incoming[s]
+        lower = lower + pltpu.roll(jnp.where(low, got, 0.0), s * (cols // 2), 1)
+        upper = upper + pltpu.roll(jnp.where(low, 0.0, got), (half + s * (cols // 2) - width // 2) % half, 1)
+    out_ref[...] = jnp.concatenate([lower, upper], axis=1)
 
     for side, edges, inners, passed in halos:
         for part in (side, edges, inners[0], inners[1], passed):
@@ -351,8 +358,9 @@
     tokens = area // 4
     f, w, h = np.meshgrid(np.arange(frames), np.arange(cols), np.arange(rows), indexing="ij")
     line = f * (rows // 2) + h // 2
-    target = (line // per) * area + (2 * (h % 2) + w % 2) * tokens + (line % per) * (n * cols // 2) + w // 2
-    place = (target.reshape(-1, 1) == np.arange(n * area)[None]).astype(ml_dtypes.bfloat16)
+    width = n * cols // 2
+    target = (line // per) * (area // 2) + (h % 2) * (width // 2) + (w % 2) * tokens + (line % per) * width + w // 2
+    place = (target.reshape(-1, 1) == np.arange(n * area // 2)[None]).astype(ml_dtypes.bfloat16)
 
     bf16, f32 = jnp.bfloat16, jnp.float32
     vmem = pl.BlockSpec(memory_space=pltpu.VMEM)
@@ -372,15 +380,15 @@
             pltpu.VMEM((2, frames, rows * cols, chans), f32),
             grid_buf, grid_buf, grid_buf, kernel_buf, kernel_buf,
             pltpu.VMEM((chans, chans), bf16),
-            pltpu.VMEM((area, n * area), bf16),
+            pltpu.VMEM((area, n * area // 2), bf16),
             pltpu.VMEM((3 * chans, area), f32),
             plane, plane, plane,
             pltpu.VMEM((n, stat, chans), f32),
             pltpu.VMEM((stat, chans), f32),
             pltpu.VMEM((n, 2 * frames, chans), f32),
             pltpu.VMEM((n, 2 * frames, chans), f32),
-            pltpu.VMEM((n, lat, area), f32),
-            pltpu.VMEM((n, lat, area), f32),
+            pltpu.VMEM((n, lat, area // 2), f32),
+            pltpu.VMEM((n, lat, area // 2), f32),
             dma((2, 3, 3)), dma((5,)), dma((3, 8)), dma((3, 8)),
             dma((3, n)), dma((3, n)), dma((1, n)), dma((1, n)),
         ],

time: 51.2 us -> 50.4 us (0.984)
  Pallas kernels: 49.6 us -> 48.8 us
    pallas_call x1, Pallas kernels: 49.6 us -> 48.8 us  [shards(): pl.pallas_call(functools.partial(body, n_tm, n), out_shape=jax.ShapeDtype...]
where the time goes in v3:
time: 50.4 us; the launch traced here: 50.2 us
  Pallas kernels  48.8 us (97%)
  local copies, waits for them, and re-layouts  1.4 us (3%)
    pallas_call x1, Pallas kernels, shards(): pl.pallas_call(functools.partial(body, n_tm, n), out_shape=jax.ShapeDtype...  48.8 us
    reshape x1, local copies, waits for them, and re-layouts, shards(): return out.reshape(4 * lat, tokens)  1.4 us

profile of v3, /device:TPU:0, one launch (start us, length us, event | category | flops | bytes accessed | tf_op | source)
XLA Modules:
  0.0 50.2 jit_solution(10982616143681682443)
XLA Ops:
  0.0 48.8 %shard_map.118 = f32[16,256]{1,0:T(8,128)} custom-call(f32[384]{0:T(512)} %gain2.1, f32[384]{0:T(512)} %shift2.1, f32[384]{0:T(512)} %gain1.1, f32[384]{0:T(512)} %shift1.1, bf16[27,16,384]{2,1,0:T(8,128)(2,1)} %lat_ref.1, bf16[2,32,4,384]{3,2,1,0:T(4,128)(2,1)} %g_hbm.1, bf16[2,32,4,384]{3,2,1,0:T(4,128)(2,1)} %x2_hbm.1, bf16[2,32,4,384]{3,2,1,0:T(4,128)(2,1)} %x1_hbm.1, ...), custom_call_target="tpu_custom_call" | custom-call | flops 4076863488 | bytes 15925248 | tf_op jit(solution)/shard_map/pallas_call | solution.py:373
  48.8 1.4 %reshape.11 = f32[64,64]{1,0:T(8,128)} reshape(f32[16,256]{1,0:T(8,128)} %shard_map.118) | data formatting | bytes 32768 | tf_op jit(solution)/shard_map/reshape | solution.py:407

commit v4 on v3

--- a/solution.py
+++ b/solution.py
@@ -210,35 +210,37 @@
     lane_h = lax.rem(lax.broadcasted_iota(jnp.int32, (chans, spot), 1), rows)
     not_last, not_first = lane_h < rows - 1, lane_h > 0
 
-    def frames_ready(moves, step):
+    groups = [[(2, 1)], [(2, 0), (2, 2)], [(1, 1), (0, 1)], [(1, 0), (1, 2), (0, 0), (0, 2)]]
+
+    def group_ready(moves, step, between=lambda: None):
         side, edges, inners, passed = moves
-        if step == 0:
+        if step == 1:
             arrive(side)
-        elif step == 1:
+        elif step == 2:
+            arrive(edges)
+            start(passed)
+            between()
             arrive(inners[0])
+            arrive(inners[1])
+        elif step == 3:
             arrive(passed)
-        else:
-            arrive(inners[1])
-
-    def pass_on(moves):
-        arrive(moves[1])
-        start(moves[3])
+
+    def pixels_of(buf, pairs):
+        return jnp.concatenate(
+            [buf[2 - a : 2 - a + frames, 2 - c : 2 - c + cols].reshape(area, chans) for a, c in pairs], axis=1
+        )
 
     def conv(buf, kb, k_hbm, which, moves, between):
-        for step, a in enumerate((2, 1, 0)):
-            frames_ready(moves, step)
-            for c in range(3):
+        for step, pairs in enumerate(groups):
+            group_ready(moves, step, between)
+            for a, c in pairs:
                 load(k_hbm, kb, which, a, c).wait()
-            pixels = jnp.concatenate(
-                [buf[2 - a : 2 - a + frames, 2 - c : 2 - c + cols].reshape(area, chans) for c in range(3)],
+            weights = jnp.concatenate(
+                [kb[3 * a : 3 * a + 3, :, c * chans : (c + 1) * chans].reshape(3 * chans, chans) for a, c in pairs],
                 axis=1,
             )
-            weights = kb[3 * a : 3 * a + 3].reshape(3 * chans, 3 * chans)
-            part = lax.dot_general(weights, pixels, NT, preferred_element_type=f32)
+            part = lax.dot_general(weights, pixels_of(buf, pairs), NT, preferred_element_type=f32)
             acc[...] = part if step == 0 else acc[...] + part
-            if step == 0:
-                pass_on(moves)
-                between()
 
     def section(k, gain, shift, buf, nxt, kb, k_hbm, moves, sums, index, next_moves):
         inv = []
@@ -295,20 +297,13 @@
     moves1 = section(1, as_row(gain1), as_row(shift1), g2, g3, kb1, k1_hbm, halos[1], sums1, 2, halos[2])
 
     result = None
-    for step, a in enumerate((2, 1, 0)):
-        frames_ready(halos[2], step)
+    for step, pairs in enumerate(groups):
+        group_ready(halos[2], step)
         weights = jnp.concatenate(
-            [jnp.concatenate([lat_ref[9 * a + 3 * b + c] for c in range(3)], axis=1) for b in range(3)],
-            axis=0,
+            [jnp.concatenate([lat_ref[9 * a + 3 * b + c] for a, c in pairs], axis=1) for b in range(3)], axis=0
         )
-        pixels = jnp.concatenate(
-            [g3[2 - a : 2 - a + frames, 2 - c : 2 - c + cols].reshape(area, chans) for c in range(3)],
-            axis=1,
-        )
-        part = lax.dot_general(weights, pixels, NT, preferred_element_type=f32)
+        part = lax.dot_general(weights, pixels_of(g3, pairs), NT, preferred_element_type=f32)
         result = part if result is None else result + part
-        if step == 0:
-            pass_on(halos[2])
     lane = lax.broadcasted_iota(jnp.int32, (lat, area), 1)
     lane_row = lax.rem(lane, rows)
     up = jnp.where(lane_row < rows - 1, pltpu.roll(result[:lat], area - 1, 1), 0.0)

time: 50.4 us -> 48.3 us (0.958)
  Pallas kernels: 48.8 us -> 46.7 us
    pallas_call x1, Pallas kernels: 48.8 us -> 46.7 us  [shards(): pl.pallas_call(functools.partial(body, n_tm, n), out_shape=jax.ShapeDtype...]
where the time goes in v4:
time: 48.3 us; the launch traced here: 48.1 us
  Pallas kernels  46.7 us (97%)
  local copies, waits for them, and re-layouts  1.4 us (3%)
    pallas_call x1, Pallas kernels, shards(): pl.pallas_call(functools.partial(body, n_tm, n), out_shape=jax.ShapeDtype...  46.7 us
    reshape x1, local copies, waits for them, and re-layouts, shards(): return out.reshape(4 * lat, tokens)  1.4 us

profile of v4, /device:TPU:0, one launch (start us, length us, event | category | flops | bytes accessed | tf_op | source)
XLA Modules:
  0.0 48.1 jit_solution(2385813071111985950)
XLA Ops:
  0.0 46.7 %shard_map.118 = f32[16,256]{1,0:T(8,128)} custom-call(f32[384]{0:T(512)} %gain2.1, f32[384]{0:T(512)} %shift2.1, f32[384]{0:T(512)} %gain1.1, f32[384]{0:T(512)} %shift1.1, bf16[27,16,384]{2,1,0:T(8,128)(2,1)} %lat_ref.1, bf16[2,32,4,384]{3,2,1,0:T(4,128)(2,1)} %g_hbm.1, bf16[2,32,4,384]{3,2,1,0:T(4,128)(2,1)} %x2_hbm.1, bf16[2,32,4,384]{3,2,1,0:T(4,128)(2,1)} %x1_hbm.1, ...), custom_call_target="tpu_custom_call" | custom-call | flops 4076863488 | bytes 15925248 | tf_op jit(solution)/shard_map/pallas_call | solution.py:368
  46.7 1.4 %reshape.11 = f32[64,64]{1,0:T(8,128)} reshape(f32[16,256]{1,0:T(8,128)} %shard_map.118) | data formatting | bytes 32768 | tf_op jit(solution)/shard_map/reshape | solution.py:402

commit v5 on v4

--- a/solution.py
+++ b/solution.py
@@ -34,9 +34,9 @@
     gain2, shift2, gain1, shift1, lat_ref,
     g_hbm, x2_hbm, x1_hbm, k2_hbm, k1_hbm, group_hbm, place_hbm,
     out_ref,
-    raw, x_s, g1, g2, g3, kb2, kb1, group_m, place_m, acc, xhat_s, coef_s, q_s,
+    raw, x_s, x_b, x_e, q_e, g1, g2, g3, kb2, kb1, group_m, place_m, acc, xhat_s, coef_s, q_s,
     mom, mom_all, sums2, sums1, outgoing, incoming,
-    k_sem, c_sem, halo_send, halo_recv, st_send, st_recv, a_send, a_recv,
+    k_sem, c_sem, halo_send, halo_recv, e_send, e_recv, st_send, st_recv, a_send, a_recv,
 ):
     tm = lax.axis_index("tm")
     me = lax.axis_index("tile")
@@ -116,6 +116,7 @@
         for f in range(frames):
             x = turned(1 + k, f)
             x_s[k, f] = x
+            x_b[k, f] = x.astype(jnp.bfloat16).reshape(cols, rows, chans)
             at = 2 * frames * k + 2 * f
             mom[me, pl.ds(at, 1)] = jnp.sum(x, axis=0, keepdims=True)
             mom[me, pl.ds(at + 1, 1)] = jnp.sum(x * x, axis=0, keepdims=True)
@@ -150,7 +151,30 @@
             (copy(buf.at[next_two, 1], buf.at[next_two, cols + 1], 7, 0, -1),
              both(has_f, has_l), both(has_f, has_r)),
         ]
-        return side, edges, inners, passed
+        return (side if stage == 0 else []), edges, inners, passed
+
+    def edge_moves(src_last, src_first, dst, at):
+        def copy(src, to, slot, dw):
+            return pltpu.make_async_remote_copy(
+                src_ref=src, dst_ref=to, send_sem=e_send.at[slot], recv_sem=e_recv.at[slot],
+                device_id={"tm": tm, "tile": me + dw}, device_id_type=MESH,
+            )
+
+        return [
+            (copy(src_last, dst.at[0], at, 1), has_r, has_l),
+            (copy(src_first, dst.at[1], at + 1, -1), has_l, has_r),
+        ]
+
+    every = pl.ds(0, frames)
+    x_edges = [
+        edge_moves(x_b.at[k, every, cols - 1], x_b.at[k, every, 0], x_e.at[k], 2 * k) for k in range(2)
+    ]
+    q_edges = [
+        edge_moves(
+            q_s.at[k, every, pl.ds(spot - rows, rows)], q_s.at[k, every, pl.ds(0, rows)], q_e.at[k], 4 + 2 * k
+        )
+        for k in range(2)
+    ]
 
     def start(moves):
         for move, sends, _ in moves:
@@ -206,6 +230,8 @@
     for a in (1, 0):
         for c in range(3):
             load(k2_hbm, kb2, 0, a, c).start()
+    for k in range(2):
+        start(x_edges[k])
 
     lane_h = lax.rem(lax.broadcasted_iota(jnp.int32, (chans, spot), 1), rows)
     not_last, not_first = lane_h < rows - 1, lane_h > 0
@@ -243,7 +269,7 @@
             acc[...] = part if step == 0 else acc[...] + part
 
     def section(k, gain, shift, buf, nxt, kb, k_hbm, moves, sums, index, next_moves):
-        inv = []
+        inv, averages = [], []
 
         def factors():
             if k == 0:
@@ -261,6 +287,7 @@
                 var = mom_all[at + 1 : at + 2] / cells - mean * mean
                 r = lax.rsqrt(var + epsilon)
                 inv.append(r)
+                averages.append(mean)
                 xhat = (x_s[k, f] - mean) * r
                 z = xhat * gain + shift
                 sig = jax.nn.sigmoid(z)
@@ -273,21 +300,32 @@
             up = jnp.where(not_last, pltpu.roll(acc[:chans, at], spot - 1, 1), 0.0)
             down = jnp.where(not_first, pltpu.roll(acc[2 * chans :, at], 1, 1), 0.0)
             q = (up + acc[chans : 2 * chans, at] + down).T * coef_s[f]
-            q_s[f] = q
+            q_s[k, f] = q
             sums[me, pl.ds(2 * f, 1)] = jnp.sum(q, axis=0, keepdims=True)
             sums[me, pl.ds(2 * f + 1, 1)] = jnp.sum(q * xhat_s[f], axis=0, keepdims=True)
         sum_moves = spread(sums, st_send, st_recv, index)
         for move, _ in sum_moves:
             move.start()
+        start(q_edges[k])
         for _, move in sum_moves:
             move.wait_recv()
         means = times_exact(total(sums), group_m[...]) / cells
         for f in range(frames):
             m1, m2 = means[2 * f : 2 * f + 1], means[2 * f + 1 : 2 * f + 2]
             own = buf[f, 1 : 1 + cols].reshape(spot, chans).astype(f32)
-            dx = own + inv[f] * (q_s[f] - m1 - xhat_s[f] * m2)
+            dx = own + inv[f] * (q_s[k, f] - m1 - xhat_s[f] * m2)
             nxt[f, 1 : 1 + cols] = dx.astype(jnp.bfloat16).reshape(cols, rows, chans)
         send_own(next_moves)
+        arrive(x_edges[k])
+        arrive(q_edges[k])
+        for at, (col, there) in enumerate(((0, has_l), (cols + 1, has_r))):
+            @pl.when(there)
+            def _():
+                for f in range(frames):
+                    m1, m2 = means[2 * f : 2 * f + 1], means[2 * f + 1 : 2 * f + 2]
+                    xhat = (x_e[k, at, f].astype(f32) - averages[f]) * inv[f]
+                    dx = buf[f, col].astype(f32) + inv[f] * (q_e[k, at, f] - m1 - xhat * m2)
+                    nxt[f, col] = dx.astype(jnp.bfloat16)
         return sum_moves
 
     def as_row(ref):
@@ -332,6 +370,8 @@
     for side, edges, inners, passed in halos:
         for part in (side, edges, inners[0], inners[1], passed):
             sent(part)
+    for moves in (*x_edges, *q_edges):
+        sent(moves)
     for moves in (mom_moves, moves2, moves1, last):
         for move, _ in moves:
             move.wait_send()
@@ -373,18 +413,21 @@
         scratch_shapes=[
             pltpu.VMEM((3, frames, rows, cols, chans), bf16),
             pltpu.VMEM((2, frames, rows * cols, chans), f32),
+            pltpu.VMEM((2, frames, cols, rows, chans), bf16),
+            pltpu.VMEM((2, 2, frames, rows, chans), bf16),
+            pltpu.VMEM((2, 2, frames, rows, chans), f32),
             grid_buf, grid_buf, grid_buf, kernel_buf, kernel_buf,
             pltpu.VMEM((chans, chans), bf16),
             pltpu.VMEM((area, n * area // 2), bf16),
             pltpu.VMEM((3 * chans, area), f32),
-            plane, plane, plane,
+            plane, plane, pltpu.VMEM((2, frames, cols * rows, chans), f32),
             pltpu.VMEM((n, stat, chans), f32),
             pltpu.VMEM((stat, chans), f32),
             pltpu.VMEM((n, 2 * frames, chans), f32),
             pltpu.VMEM((n, 2 * frames, chans), f32),
             pltpu.VMEM((n, lat, area // 2), f32),
             pltpu.VMEM((n, lat, area // 2), f32),
-            dma((2, 3, 3)), dma((5,)), dma((3, 8)), dma((3, 8)),
+            dma((2, 3, 3)), dma((5,)), dma((3, 8)), dma((3, 8)), dma((8,)), dma((8,)),
             dma((3, n)), dma((3, n)), dma((1, n)), dma((1, n)),
         ],
         compiler_params=pltpu.CompilerParams(

time: 48.3 us -> 49 us (1.014)
  Pallas kernels: 46.7 us -> 47.3 us
    pallas_call x1, Pallas kernels: 46.7 us -> 47.3 us  [shards(): pl.pallas_call(functools.partial(body, n_tm, n), out_shape=jax.ShapeDtype...]
where the time goes in v5:
time: 49 us; the launch traced here: 48.7 us
  Pallas kernels  47.3 us (97%)
  local copies, waits for them, and re-layouts  1.4 us (3%)
    pallas_call x1, Pallas kernels, shards(): pl.pallas_call(functools.partial(body, n_tm, n), out_shape=jax.ShapeDtype...  47.3 us
    reshape x1, local copies, waits for them, and re-layouts, shards(): return out.reshape(4 * lat, tokens)  1.4 us

profile of v5, /device:TPU:0, one launch (start us, length us, event | category | flops | bytes accessed | tf_op | source)
XLA Modules:
  0.0 48.7 jit_solution(4426955621246598296)
XLA Ops:
  0.0 47.3 %shard_map.118 = f32[16,256]{1,0:T(8,128)} custom-call(f32[384]{0:T(512)} %gain2.1, f32[384]{0:T(512)} %shift2.1, f32[384]{0:T(512)} %gain1.1, f32[384]{0:T(512)} %shift1.1, bf16[27,16,384]{2,1,0:T(8,128)(2,1)} %lat_ref.1, bf16[2,32,4,384]{3,2,1,0:T(4,128)(2,1)} %g_hbm.1, bf16[2,32,4,384]{3,2,1,0:T(4,128)(2,1)} %x2_hbm.1, bf16[2,32,4,384]{3,2,1,0:T(4,128)(2,1)} %x1_hbm.1, ...), custom_call_target="tpu_custom_call" | custom-call | flops 4076863488 | bytes 15925248 | tf_op jit(solution)/shard_map/pallas_call | solution.py:408
  47.3 1.4 %reshape.11 = f32[64,64]{1,0:T(8,128)} reshape(f32[16,256]{1,0:T(8,128)} %shard_map.118) | data formatting | bytes 32768 | tf_op jit(solution)/shard_map/reshape | solution.py:445

commit v6 on v5

--- a/solution.py
+++ b/solution.py
@@ -34,7 +34,7 @@
     gain2, shift2, gain1, shift1, lat_ref,
     g_hbm, x2_hbm, x1_hbm, k2_hbm, k1_hbm, group_hbm, place_hbm,
     out_ref,
-    raw, x_s, x_b, x_e, q_e, g1, g2, g3, kb2, kb1, group_m, place_m, acc, xhat_s, coef_s, q_s,
+    raw, x_s, x_b, x_e, q_e, x_f, q_b, q_f, norm_out, norm_in, g1, g2, g3, kb2, kb1, group_m, place_m, acc, xhat_s, coef_s, q_s,
     mom, mom_all, sums2, sums1, outgoing, incoming,
     k_sem, c_sem, halo_send, halo_recv, e_send, e_recv, st_send, st_recv, a_send, a_recv,
 ):
@@ -151,7 +151,9 @@
             (copy(buf.at[next_two, 1], buf.at[next_two, cols + 1], 7, 0, -1),
              both(has_f, has_l), both(has_f, has_r)),
         ]
-        return (side if stage == 0 else []), edges, inners, passed
+        if stage:
+            return [], [], [[], []], passed
+        return side, edges, inners, passed
 
     def edge_moves(src_last, src_first, dst, at):
         def copy(src, to, slot, dw):
@@ -164,6 +166,18 @@
             (copy(src_last, dst.at[0], at, 1), has_r, has_l),
             (copy(src_first, dst.at[1], at + 1, -1), has_l, has_r),
         ]
+
+    def next_move(src, dst, k, slot):
+        move = pltpu.make_async_remote_copy(
+            src_ref=src, dst_ref=dst,
+            send_sem=halo_send.at[k + 1, slot], recv_sem=halo_recv.at[k + 1, slot],
+            device_id={"tm": tm - 1, "tile": me}, device_id_type=MESH,
+        )
+        return (move, has_p, has_f)
+
+    x_next = [[next_move(x_b.at[k, pl.ds(0, 2)], x_f.at[k], k, 5)] for k in range(2)]
+    q_next = [[next_move(q_b.at[k, f], q_f.at[k, f], k, 2 + f) for f in range(2)] for k in range(2)]
+    norm_next = [[next_move(norm_out.at[k], norm_in.at[k], k, 4)] for k in range(2)]
 
     every = pl.ds(0, frames)
     x_edges = [
@@ -214,11 +228,6 @@
         return out
 
     halos = [halo(buf, i) for i, buf in enumerate((g1, g2, g3))]
-    def send_own(moves):
-        start(moves[0])
-        start(moves[1])
-        for part in moves[2]:
-            start(part)
 
     mom_moves = spread(mom, st_send, st_recv, 0)
     start(halos[0][0])
@@ -232,33 +241,37 @@
             load(k2_hbm, kb2, 0, a, c).start()
     for k in range(2):
         start(x_edges[k])
+        start(x_next[k])
 
     lane_h = lax.rem(lax.broadcasted_iota(jnp.int32, (chans, spot), 1), rows)
     not_last, not_first = lane_h < rows - 1, lane_h > 0
 
-    groups = [[(2, 1)], [(2, 0), (2, 2)], [(1, 1), (0, 1)], [(1, 0), (1, 2), (0, 0), (0, 2)]]
-
-    def group_ready(moves, step, between=lambda: None):
+    first_groups = [[(2, 1)], [(2, 0), (2, 2)], [(1, 1)], [(1, 0), (1, 2)], [(0, 1), (0, 0), (0, 2)]]
+    later_groups = [[(2, 1)], [(2, 0), (2, 2)], [(1, 1), (0, 1)], [(1, 0), (1, 2), (0, 0), (0, 2)]]
+
+    def group_ready(moves, step, form, between=lambda: None):
         side, edges, inners, passed = moves
         if step == 1:
             arrive(side)
         elif step == 2:
             arrive(edges)
+            form()
             start(passed)
             between()
             arrive(inners[0])
-            arrive(inners[1])
         elif step == 3:
             arrive(passed)
+        elif step == 4:
+            arrive(inners[1])
 
     def pixels_of(buf, pairs):
         return jnp.concatenate(
             [buf[2 - a : 2 - a + frames, 2 - c : 2 - c + cols].reshape(area, chans) for a, c in pairs], axis=1
         )
 
-    def conv(buf, kb, k_hbm, which, moves, between):
-        for step, pairs in enumerate(groups):
-            group_ready(moves, step, between)
+    def conv(buf, kb, k_hbm, which, moves, form, between):
+        for step, pairs in enumerate(later_groups if which else first_groups):
+            group_ready(moves, step, form, between)
             for a, c in pairs:
                 load(k_hbm, kb, which, a, c).wait()
             weights = jnp.concatenate(
@@ -268,7 +281,7 @@
             part = lax.dot_general(weights, pixels_of(buf, pairs), NT, preferred_element_type=f32)
             acc[...] = part if step == 0 else acc[...] + part
 
-    def section(k, gain, shift, buf, nxt, kb, k_hbm, moves, sums, index, next_moves):
+    def section(k, gain, shift, buf, nxt, kb, k_hbm, moves, form, sums, index):
         inv, averages = [], []
 
         def factors():
@@ -294,28 +307,34 @@
                 xhat_s[f] = xhat
                 coef_s[f] = sig * (1.0 + z * (1.0 - sig)) * gain
 
-        conv(buf, kb, k_hbm, k, moves, factors)
+        conv(buf, kb, k_hbm, k, moves, form, factors)
         for f in range(frames):
             at = pl.ds(f * spot, spot)
             up = jnp.where(not_last, pltpu.roll(acc[:chans, at], spot - 1, 1), 0.0)
             down = jnp.where(not_first, pltpu.roll(acc[2 * chans :, at], 1, 1), 0.0)
             q = (up + acc[chans : 2 * chans, at] + down).T * coef_s[f]
             q_s[k, f] = q
+            if f < 2:
+                q_b[k, f] = q.astype(jnp.bfloat16).reshape(cols, rows, chans)
             sums[me, pl.ds(2 * f, 1)] = jnp.sum(q, axis=0, keepdims=True)
             sums[me, pl.ds(2 * f + 1, 1)] = jnp.sum(q * xhat_s[f], axis=0, keepdims=True)
         sum_moves = spread(sums, st_send, st_recv, index)
         for move, _ in sum_moves:
             move.start()
         start(q_edges[k])
+        start(q_next[k])
         for _, move in sum_moves:
             move.wait_recv()
         means = times_exact(total(sums), group_m[...]) / cells
+        for f in range(2):
+            for i, row in enumerate((averages[f], inv[f], means[2 * f : 2 * f + 1], means[2 * f + 1 : 2 * f + 2])):
+                norm_out[k, pl.ds(4 * f + i, 1)] = row
+        start(norm_next[k])
         for f in range(frames):
             m1, m2 = means[2 * f : 2 * f + 1], means[2 * f + 1 : 2 * f + 2]
             own = buf[f, 1 : 1 + cols].reshape(spot, chans).astype(f32)
             dx = own + inv[f] * (q_s[k, f] - m1 - xhat_s[f] * m2)
             nxt[f, 1 : 1 + cols] = dx.astype(jnp.bfloat16).reshape(cols, rows, chans)
-        send_own(next_moves)
         arrive(x_edges[k])
         arrive(q_edges[k])
         for at, (col, there) in enumerate(((0, has_l), (cols + 1, has_r))):
@@ -326,17 +345,34 @@
                     xhat = (x_e[k, at, f].astype(f32) - averages[f]) * inv[f]
                     dx = buf[f, col].astype(f32) + inv[f] * (q_e[k, at, f] - m1 - xhat * m2)
                     nxt[f, col] = dx.astype(jnp.bfloat16)
-        return sum_moves
+
+        def form_next():
+            arrive(x_next[k])
+            arrive(q_next[k])
+            arrive(norm_next[k])
+
+            @pl.when(has_f)
+            def _():
+                for f in range(2):
+                    mean, r, m1, m2 = (norm_in[k, 4 * f + i : 4 * f + i + 1] for i in range(4))
+                    xhat = (x_f[k, f].reshape(spot, chans).astype(f32) - mean) * r
+                    g = buf[frames + f, 1 : 1 + cols].reshape(spot, chans).astype(f32)
+                    dx = g + r * (q_f[k, f].reshape(spot, chans).astype(f32) - m1 - xhat * m2)
+                    nxt[frames + f, 1 : 1 + cols] = dx.astype(jnp.bfloat16).reshape(cols, rows, chans)
+
+        return sum_moves, form_next
 
     def as_row(ref):
         return ref[...].reshape(1, chans)
 
-    moves2 = section(0, as_row(gain2), as_row(shift2), g1, g2, kb2, k2_hbm, halos[0], sums2, 1, halos[1])
-    moves1 = section(1, as_row(gain1), as_row(shift1), g2, g3, kb1, k1_hbm, halos[1], sums1, 2, halos[2])
+    moves2, form2 = section(
+        0, as_row(gain2), as_row(shift2), g1, g2, kb2, k2_hbm, halos[0], lambda: None, sums2, 1
+    )
+    moves1, form1 = section(1, as_row(gain1), as_row(shift1), g2, g3, kb1, k1_hbm, halos[1], form2, sums1, 2)
 
     result = None
-    for step, pairs in enumerate(groups):
-        group_ready(halos[2], step)
+    for step, pairs in enumerate(later_groups):
+        group_ready(halos[2], step, form1)
         weights = jnp.concatenate(
             [jnp.concatenate([lat_ref[9 * a + 3 * b + c] for a, c in pairs], axis=1) for b in range(3)], axis=0
         )
@@ -370,7 +406,7 @@
     for side, edges, inners, passed in halos:
         for part in (side, edges, inners[0], inners[1], passed):
             sent(part)
-    for moves in (*x_edges, *q_edges):
+    for moves in (*x_edges, *q_edges, *x_next, *q_next, *norm_next):
         sent(moves)
     for moves in (mom_moves, moves2, moves1, last):
         for move, _ in moves:
@@ -403,6 +439,7 @@
     grid_buf = pltpu.VMEM((frames + 2, cols + 2, rows, chans), bf16)
     kernel_buf = pltpu.VMEM((9, chans, 3 * chans), bf16)
     plane = pltpu.VMEM((frames, cols * rows, chans), f32)
+    next_buf = pltpu.VMEM((2, 2, cols, rows, chans), bf16)
     stat = -(-4 * frames // 8) * 8
     dma = pltpu.SemaphoreType.DMA
     out = pl.pallas_call(
@@ -416,6 +453,9 @@
             pltpu.VMEM((2, frames, cols, rows, chans), bf16),
             pltpu.VMEM((2, 2, frames, rows, chans), bf16),
             pltpu.VMEM((2, 2, frames, rows, chans), f32),
+            next_buf, next_buf, next_buf,
+            pltpu.VMEM((2, 8, chans), f32),
+            pltpu.VMEM((2, 8, chans), f32),
             grid_buf, grid_buf, grid_buf, kernel_buf, kernel_buf,
             pltpu.VMEM((chans, chans), bf16),
             pltpu.VMEM((area, n * area // 2), bf16),

time: 49 us -> 48 us (0.980)
  Pallas kernels: 47.3 us -> 46.4 us
    pallas_call x1, Pallas kernels: 47.3 us -> 46.4 us  [shards(): pl.pallas_call(functools.partial(body, n_tm, n), out_shape=jax.ShapeDtype...]
where the time goes in v6:
time: 48 us; the launch traced here: 47.8 us
  Pallas kernels  46.4 us (97%)
  local copies, waits for them, and re-layouts  1.4 us (3%)
    pallas_call x1, Pallas kernels, shards(): pl.pallas_call(functools.partial(body, n_tm, n), out_shape=jax.ShapeDtype...  46.4 us
    reshape x1, local copies, waits for them, and re-layouts, shards(): return out.reshape(4 * lat, tokens)  1.4 us

profile of v6, /device:TPU:0, one launch (start us, length us, event | category | flops | bytes accessed | tf_op | source)
XLA Modules:
  0.0 47.8 jit_solution(15134188462517929220)
XLA Ops:
  0.0 46.4 %shard_map.118 = f32[16,256]{1,0:T(8,128)} custom-call(f32[384]{0:T(512)} %gain2.1, f32[384]{0:T(512)} %shift2.1, f32[384]{0:T(512)} %gain1.1, f32[384]{0:T(512)} %shift1.1, bf16[27,16,384]{2,1,0:T(8,128)(2,1)} %lat_ref.1, bf16[2,32,4,384]{3,2,1,0:T(4,128)(2,1)} %g_hbm.1, bf16[2,32,4,384]{3,2,1,0:T(4,128)(2,1)} %x2_hbm.1, bf16[2,32,4,384]{3,2,1,0:T(4,128)(2,1)} %x1_hbm.1, ...), custom_call_target="tpu_custom_call" | custom-call | flops 4076863488 | bytes 15925248 | tf_op jit(solution)/shard_map/pallas_call | solution.py:445
  46.4 1.4 %reshape.11 = f32[64,64]{1,0:T(8,128)} reshape(f32[16,256]{1,0:T(8,128)} %shard_map.118) | data formatting | bytes 32768 | tf_op jit(solution)/shard_map/reshape | solution.py:485

commit v7 on v6

--- a/solution.py
+++ b/solution.py
@@ -241,7 +241,6 @@
             load(k2_hbm, kb2, 0, a, c).start()
     for k in range(2):
         start(x_edges[k])
-        start(x_next[k])
 
     lane_h = lax.rem(lax.broadcasted_iota(jnp.int32, (chans, spot), 1), rows)
     not_last, not_first = lane_h < rows - 1, lane_h > 0
@@ -294,6 +293,8 @@
                 const_loads[1].start()
                 const_loads[0].wait()
                 mom_all[...] = times_exact(total(mom), group_m[...])
+            else:
+                start(x_next[1])
             for f in range(frames):
                 at = 2 * frames * k + 2 * f
                 mean = mom_all[at : at + 1] / cells
@@ -308,6 +309,8 @@
                 coef_s[f] = sig * (1.0 + z * (1.0 - sig)) * gain
 
         conv(buf, kb, k_hbm, k, moves, form, factors)
+        if k == 0:
+            start(x_next[0])
         for f in range(frames):
             at = pl.ds(f * spot, spot)
             up = jnp.where(not_last, pltpu.roll(acc[:chans, at], spot - 1, 1), 0.0)

time: 48 us -> 49.6 us (1.033)
  Pallas kernels: 46.4 us -> 47.9 us
    pallas_call x1, Pallas kernels: 46.4 us -> 47.9 us  [shards(): pl.pallas_call(functools.partial(body, n_tm, n), out_shape=jax.ShapeDtype...]
where the time goes in v7:
time: 49.6 us; the launch traced here: 49.3 us
  Pallas kernels  47.9 us (97%)
  local copies, waits for them, and re-layouts  1.4 us (3%)
    pallas_call x1, Pallas kernels, shards(): pl.pallas_call(functools.partial(body, n_tm, n), out_shape=jax.ShapeDtype...  47.9 us
    reshape x1, local copies, waits for them, and re-layouts, shards(): return out.reshape(4 * lat, tokens)  1.4 us

profile of v7, /device:TPU:0, one launch (start us, length us, event | category | flops | bytes accessed | tf_op | source)
XLA Modules:
  0.0 49.3 jit_solution(10190776968137020243)
XLA Ops:
  0.0 47.9 %shard_map.118 = f32[16,256]{1,0:T(8,128)} custom-call(f32[384]{0:T(512)} %gain2.1, f32[384]{0:T(512)} %shift2.1, f32[384]{0:T(512)} %gain1.1, f32[384]{0:T(512)} %shift1.1, bf16[27,16,384]{2,1,0:T(8,128)(2,1)} %lat_ref.1, bf16[2,32,4,384]{3,2,1,0:T(4,128)(2,1)} %g_hbm.1, bf16[2,32,4,384]{3,2,1,0:T(4,128)(2,1)} %x2_hbm.1, bf16[2,32,4,384]{3,2,1,0:T(4,128)(2,1)} %x1_hbm.1, ...), custom_call_target="tpu_custom_call" | custom-call | flops 4076863488 | bytes 15925248 | tf_op jit(solution)/shard_map/pallas_call | solution.py:448
  47.9 1.4 %reshape.11 = f32[64,64]{1,0:T(8,128)} reshape(f32[16,256]{1,0:T(8,128)} %shard_map.118) | data formatting | bytes 32768 | tf_op jit(solution)/shard_map/reshape | solution.py:488
